TPU v7x, 32 devices: a whole 2x2x4 slice. The times are simulated.
32 devices in a mesh: grp: 4 (over y, x), mem: 8 (over z, core).
Axes of the slice: x: 2, y: 2, z: 4, core: 2. Of those that a mesh axis runs over, the one named last changes fastest.
Arguments:
- pno: bfloat16 [1024, 512, 128], P(('grp', 'mem')), may hold values from -0.5 to 0.5
- amplitudes: bfloat16 [1024, 128, 128], P(('grp', 'mem')), may hold values from -6 to 6
- pno_count: int32 [1024], P(('grp', 'mem')), may hold values from 64 to 128
- pao_coupling: bfloat16 [512, 512], replicated, may hold values from -0.25 to 0.25
- row_owner: int32 [2048, 1], P(('grp', 'mem')), may hold values from 0 to 7; in each aligned block of 64 rows (0 to 63, 64 to 127, ...) at most 16 rows name the same one
- row_pair: int32 [2048], P(('grp', 'mem')), may hold values from 0 to 31
- row_target: int32 [2048], P(('grp', 'mem')), may hold values from 0 to 31
- row_coef: float32 [2048], P(('grp', 'mem')), may hold values from -6 to 6
- column_owner: int32 [512, 1], P(('grp', 'mem')), may hold values from 0 to 3; in each aligned block of 16 rows (0 to 15, 16 to 31, ...) at most 8 rows name the same one
- column_pair: int32 [512], P(('grp', 'mem')), may hold values from 0 to 31
- column_target: int32 [512], P(('grp', 'mem')), may hold values from 0 to 31
- column_coef: float32 [512], P(('grp', 'mem')), may hold values from -6 to 6
Outputs:
- coupling_residual: float32 [1024, 128, 128], P(('grp', 'mem'))
Inputs may be any that keep to these rules, and one draw needn't show every extreme that they name: `row_owner`: among one device's in-group couplings at most 16 name the same member index, and some device's rows reach it. `column_owner`: among one device's cross-group couplings at most 8 name the same group index, and some device's rows reach it.
All inputs are finite; a program needn't handle non-finite values.
Results may differ from a plain program's by a relative error of at most 0.0064.
Values may be sent and summed in bfloat16 or wider, within the bound.
No kernel may reach another device: no remote copies, remote signals or barrier semaphores. Data moves between devices by JAX's collectives and lax.ppermute only.
A program may use at most 128 MiB of HBM per device.

v0:
```python
import functools

import jax
import jax.numpy as jnp
from jax import lax
from jax.experimental import pallas as pl
from jax.experimental.pallas import tpu as pltpu
from jax.sharding import PartitionSpec as P

UNIT = 16
PLANS = ((8, 35), (8, 37), (9, 36))
VMEM = 48 * 2**20
CROSS_AFTER = 5
ROW_BITS = 20
MANY = 8
ANY = pl.BlockSpec(memory_space=pl.ANY)
SMEM = pl.BlockSpec(memory_space=pltpu.SMEM)
IN_VMEM = pl.BlockSpec(memory_space=pltpu.VMEM)


def params():
    return pltpu.CompilerParams(vmem_limit_bytes=VMEM)


def block_kernel(count_ref, pno_ref, amp_ref, out_ref):
    step = pl.program_id(0)
    many, depth, width = pno_ref.shape
    for i in range(many):
        count = count_ref[step * many + i]
        rows = lax.broadcasted_iota(jnp.int32, (width, depth), 0)
        turned = pno_ref[i].T
        out_ref[pl.ds(i * width, width), pl.ds(0, depth)] = jnp.where(rows < count, turned, jnp.zeros_like(turned))
        down = lax.broadcasted_iota(jnp.int32, (width, width), 0)
        across = lax.broadcasted_iota(jnp.int32, (width, width), 1)
        amp = amp_ref[i]
        live = (down < count) & (across < count)
        out_ref[pl.ds(i * width, width), pl.ds(depth, width)] = jnp.where(live, amp, jnp.zeros_like(amp))


def blocks_of(pno, amplitudes, pno_count):
    pairs, depth, width = pno.shape
    many = 4
    return pl.pallas_call(
        block_kernel,
        grid=(pairs // many,),
        in_specs=[
            SMEM,
            pl.BlockSpec((many, depth, width), lambda i: (i, 0, 0)),
            pl.BlockSpec((many, width, width), lambda i: (i, 0, 0)),
        ],
        out_specs=pl.BlockSpec((many * width, depth + width), lambda i: (i, 0)),
        out_shape=jax.ShapeDtypeStruct((pairs * width, depth + width), pno.dtype),
        compiler_params=pltpu.CompilerParams(vmem_limit_bytes=60 * 2**20),
    )(pno_count, pno, amplitudes)


def metric_kernel(depth, block_ref, coupling_ref, out_ref):
    live = block_ref[:, pl.ds(0, depth)]
    mixed = jnp.dot(live, coupling_ref[...], preferred_element_type=jnp.float32)
    out_ref[...] = (live.astype(jnp.float32) + mixed).astype(out_ref.dtype)


def metric_blocks(blocks, pao_coupling):
    rows, columns = blocks.shape
    depth = pao_coupling.shape[0]
    tile = 512
    return pl.pallas_call(
        functools.partial(metric_kernel, depth),
        grid=(rows // tile,),
        in_specs=[pl.BlockSpec((tile, columns), lambda i: (i, 0)), pl.BlockSpec((depth, depth), lambda i: (0, 0))],
        out_specs=pl.BlockSpec((tile, depth), lambda i: (i, 0)),
        out_shape=jax.ShapeDtypeStruct((rows, depth), blocks.dtype),
        compiler_params=params(),
        cost_estimate=pl.CostEstimate(flops=0, bytes_accessed=20_000_000, transcendentals=0),
    )(blocks, pao_coupling)


def pick(array, index):
    return lax.dynamic_index_in_dim(array, index, 0, keepdims=False)


def starts_of(lengths, chips, delay):
    starts, ends = {}, []
    for c in range(chips - 1):
        at = jnp.zeros_like(lengths[0][chips - 1])
        for f in range(chips - 1, c, -1):
            for o in range(c, -1, -1):
                if o < c:
                    at = jnp.where(lengths[o][f] > 0, jnp.maximum(at, starts[o, f, c - 1] + delay), at)
                starts[o, f, c] = at
                at = at + lengths[o][f]
        ends.append(at)
    return starts, functools.reduce(jnp.maximum, ends)


def relay_plan(code, count, group, member, mine):
    groups, members, _ = code.shape
    pairs = count.shape[2]
    chips, items = members // 2, 2 * pairs
    chip, core = member // 2, member % 2
    ids = jnp.arange(members * pairs, dtype=jnp.int32)
    asked = jnp.any(code[..., None, :] == ids[:, None], axis=-1)
    asked = jnp.any(asked.reshape(groups, chips, 2, chips, items), axis=2)
    asked = jnp.stack([asked, asked[:, ::-1, ::-1]])
    line = jnp.arange(chips, dtype=jnp.int32)
    later = (line[:, None] > line[None, :])[:, :, None]
    far = jnp.max(jnp.where(asked & later, line[:, None, None], 0), axis=2)
    units = ((count + UNIT - 1) // UNIT).reshape(groups, chips, items)
    units = jnp.stack([units, units[:, ::-1]])
    order = far * items + (items - 1 - jnp.arange(items, dtype=jnp.int32))
    before = (order[..., None, :] > order[..., :, None]) & (far[..., None, :] > 0)
    lane = jnp.sum(before.astype(jnp.int32), axis=-1) & 1
    kind = far * 2 + lane
    ahead = before & (kind[..., None, :] == kind[..., :, None])
    prefix = jnp.sum(jnp.where(ahead, units[..., None, :], 0), axis=-1)
    kinds = jnp.arange(2 * chips, dtype=jnp.int32)
    total = jnp.sum(jnp.where(kind[..., None, :] == kinds[:, None], units[..., None, :], 0), axis=-1)
    total = total.reshape(2, groups, chips, chips, 2)
    lengths = [[total[:, :, o, f] for f in range(chips)] for o in range(chips)]
    branch, size, span = jnp.int32(len(PLANS)), jnp.int32(PLANS[-1][1]), jnp.int32(PLANS[-1][0] * PLANS[-1][1])
    for b, (rounds, width) in reversed(list(enumerate(PLANS))):
        fits = jnp.max(starts_of(lengths, chips, 2 * width)[1]) <= rounds * width
        branch, size, span = (jnp.where(fits, x, y) for x, y in ((b, branch), (width, size), (rounds * width, span)))

    def own_group(x):
        return lax.dynamic_index_in_dim(x, group, 1, keepdims=False)

    far, lane, prefix, units, total = (own_group(x) for x in (far, lane, prefix, units, total))
    lengths = [[total[:, o, f] for f in range(chips)] for o in range(chips)]
    starts = starts_of(lengths, chips, 2 * size)[0]
    none = jnp.zeros_like(lengths[0][0])
    runs = []
    most = max(c * (chips - 1 - c) for c in range(chips))
    for c in range(chips):
        own = [(starts[c, f, c], lengths[c][f], none) if f > c else (none, none, none) for f in range(1, chips)]
        passed = [(starts[o, f, c], lengths[o][f], starts[o, f, c - 1]) for o in range(c) for f in range(c + 1, chips)]
        passed += [(none, none, none)] * (most - len(passed))
        runs.append(jnp.stack([jnp.stack(r) for r in own + passed]))
    runs = jnp.stack(runs)
    outgo = jnp.stack([jnp.stack([starts[c, f, c] if f > c else none for f in range(chips)]) for c in range(chips)])
    income = jnp.stack(
        [
            jnp.stack([jnp.stack([starts[o, f, c - 1] if o < c <= f else none for f in range(chips)]) for o in range(chips)])
            for c in range(chips)
        ]
    )
    table, place, need, spot, side = [], [], [], [], []
    for d in range(2):
        at = chip if d == 0 else chips - 1 - chip
        table.append(lax.dynamic_index_in_dim(pick(runs, at)[..., d, :], core, 2, keepdims=False))
        home = pick(far[d], at)
        chosen = lax.dynamic_index_in_dim(pick(outgo, at)[:, d, :], core, 1, keepdims=False)
        first = jnp.sum(jnp.where(home[:, None] == line, chosen, 0), axis=1)
        place.append(first + pick(prefix[d], at))
        need.append(jnp.where((home > 0) & (pick(lane[d], at) == core), pick(units[d], at), 0))
        came = pick(income, at)[:, :, d, :]
        hit = (far[d][:, :, None, None] == line[:, None]) & (lane[d][:, :, None, None] == jnp.arange(2, dtype=jnp.int32))
        where = prefix[d] + jnp.sum(jnp.where(hit, came[:, None], 0), axis=(2, 3))
        spot.append(where if d == 0 else where[::-1])
        side.append(lane[d] if d == 0 else lane[d][::-1])
    stretch = span + 8
    origin = line[:, None]
    item = jnp.arange(items, dtype=jnp.int32)[None, :]
    width = mine[1]
    down = (origin > chip).astype(jnp.int32)
    lies = jnp.where(down == 1, spot[1], spot[0])
    on = jnp.where(down == 1, side[1], side[0])
    far_row = ((2 * down + (on != core)) * stretch + lies) * UNIT + (2 << ROW_BITS)
    near_row = (item % pairs) * width + ((item // pairs != core).astype(jnp.int32) << ROW_BITS)
    rows = jnp.where(origin == chip, near_row, far_row).reshape(-1)
    last = lies + units[0] - 1
    passed = sum((last >= r * size).astype(jnp.int32) for r in range(1, max(rounds for rounds, _ in PLANS)))
    ready = jnp.where(origin == chip, 0, passed + (on != core)).reshape(-1)
    found = mine[0][:, None] == ids
    location = jnp.sum(jnp.where(found, rows, 0), axis=1)
    when = jnp.sum(jnp.where(found, ready, 0), axis=1)
    return branch, jnp.stack(table), jnp.stack(place), jnp.stack(need), location, when


def ranks_of(owner):
    spots = jnp.arange(owner.shape[-1], dtype=jnp.int32)
    ahead = (owner[..., None, :] == owner[..., :, None]) & (spots[None, :] < spots[:, None])
    return jnp.sum(ahead.astype(jnp.int32), axis=-1)


def wanted_from(owner, pair, me, capacity):
    slot = jnp.where(owner == me, ranks_of(owner), capacity)
    hit = slot[:, None, :] == jnp.arange(capacity, dtype=jnp.int32)[:, None]
    return jnp.sum(jnp.where(hit, pair[:, None, :], 0), axis=-1)


def load_all(source, scratch, sem, parts=8):
    rows = source.shape[0] // parts
    return [
        pltpu.make_async_copy(source.at[pl.ds(i * rows, rows)], scratch.at[pl.ds(i * rows, rows)], sem) for i in range(parts)
    ]


def take_kernel(width, index_ref, blocks_ref, *refs):
    outs, (scratch, load, sem) = refs[:-3], refs[-3:]
    slots = outs[0].shape[0] // width
    loads = load_all(blocks_ref, scratch, load)
    for c in loads:
        c.start()
    for c in loads:
        c.wait()

    def copies(i):
        for k, out in enumerate(outs):
            row = pl.multiple_of(index_ref[k * slots + i] * width, UNIT)
            yield pltpu.make_async_copy(
                scratch.at[pl.ds(row, width)], out.at[pl.ds(pl.multiple_of(i * width, UNIT), width)], sem
            )

    @pl.loop(0, slots)
    def _(i):
        for c in copies(i):
            c.start()

    @pl.loop(0, slots)
    def _(i):
        for c in copies(i):
            c.wait()


def take(blocks, index, width, parts):
    slots = index.shape[0] // parts
    shape = jax.ShapeDtypeStruct((slots * width, blocks.shape[1]), blocks.dtype)
    return pl.pallas_call(
        functools.partial(take_kernel, width),
        in_specs=[SMEM, ANY],
        out_specs=[ANY] * parts,
        out_shape=[shape] * parts,
        scratch_shapes=[pltpu.VMEM(blocks.shape, blocks.dtype), pltpu.SemaphoreType.DMA, pltpu.SemaphoreType.DMA],
        compiler_params=params(),
        cost_estimate=pl.CostEstimate(flops=0, bytes_accessed=2 * parts * slots * width * blocks.shape[1] * 2, transcendentals=0),
    )(index, blocks)


def run_copies(runs_ref, d, r, window, size, source, base, out, sem, shift):
    first, length, back = runs_ref[d, r, 0], runs_ref[d, r, 1], runs_ref[d, r, 2]
    low = jnp.maximum(first, window * size)
    high = jnp.minimum(first + length, (window + 1) * size)
    taken = jnp.maximum(high - low, 0)
    begin = back + low - first if shift else low
    rows = taken * UNIT
    return taken, pltpu.make_async_copy(
        source.at[pl.ds(pl.multiple_of((base + jnp.maximum(begin, 0)) * UNIT, UNIT), rows)],
        out.at[pl.ds(pl.multiple_of((low - window * size) * UNIT, UNIT), rows)],
        sem,
    )


def windows(runs_ref, picks, window, size, source, bases, outs, sem, shift, act):
    for d in range(2):
        for r in picks:
            taken, copy = run_copies(runs_ref, d, r, window, size, source, bases[d], outs[d], sem, shift)

            @pl.when(taken > 0)
            def _():
                getattr(copy, act)()


def items_of(pairs, core_ref, sources, visit):
    for half, source in enumerate(sources):

        @pl.loop(0, pairs)
        def _(i):
            for d in range(2):
                visit(source, i, d, (core_ref[0] ^ half) * pairs + i)


def open_kernel(size, span, pairs, width, own, place_ref, need_ref, runs_ref, core_ref, mine_ref, other_ref, stream_ref, *refs):
    outs, (near, beside, load, sem) = refs[:-4], refs[-4:]
    loads = load_all(mine_ref, near, load) + load_all(other_ref, beside, load)
    for c in loads:
        c.start()
    for c in loads:
        c.wait()
    straight = (0, span)

    def visit(source, i, d, item):
        units = need_ref[d, item]

        @pl.when(units > 0)
        def _():
            pltpu.make_async_copy(
                source.at[pl.ds(pl.multiple_of(i * width, UNIT), units * UNIT)],
                stream_ref.at[pl.ds(pl.multiple_of((straight[d] + place_ref[d, item]) * UNIT, UNIT), units * UNIT)],
                sem,
            ).start()

    items_of(pairs, core_ref, (near, beside), visit)
    for d in range(2):
        total = sum(runs_ref[d, r, 1] for r in range(own)) * UNIT

        @pl.when(total > 0)
        def _():
            pltpu.make_async_copy(near.at[pl.ds(0, total)], stream_ref.at[pl.ds(0, total)], sem).wait()

    for act in ("start", "wait"):
        for window in range(2):
            part = [out.at[pl.ds(window * size * UNIT, size * UNIT)] for out in outs]
            windows(runs_ref, range(own), window, size, stream_ref, straight, part, sem, False, act)


def step_kernel(size, stretch, own, at, other_at, next_windows, runs_ref, stream_ref, *refs):
    refs = list(refs)
    if other_at is not None:
        refs.pop(0)
    came = [refs.pop(0), refs.pop(0)]
    other = [refs.pop(0), refs.pop(0)] if other_at is not None else []
    hold = refs.pop(0)
    arrive, rest, lay = refs[-3:]
    outs = refs[:-3]
    rows = size * UNIT

    def filed(piece, section, number, sem):
        return pltpu.make_async_copy(
            piece, hold.at[pl.ds(section * stretch * UNIT + number * rows, piece.shape[0])], sem
        )

    first = [filed(c, 2 * d, at, arrive.at[d]) for d, c in enumerate(came)]
    second = [filed(c, 2 * d + 1, other_at, rest.at[d]) for d, c in enumerate(other)]
    for c in first + second:
        c.start()
    straight, through = (0, stretch - 8), (0, 2 * stretch)

    def lay_out(passed, act):
        picks = range(own, runs_ref.shape[1]) if passed else range(own)
        for i, window in enumerate(next_windows):
            source, bases = (hold, through) if passed else (stream_ref, straight)
            windows(runs_ref, picks, window, size, source, bases, outs[2 * i : 2 * i + 2], lay, passed, act)

    lay_out(False, "start")
    for c in first:
        c.wait()
    lay_out(True, "start")
    lay_out(False, "wait")
    lay_out(True, "wait")
    for c in second:
        c.wait()


def close_kernel(size, stretch, number, came_up, came_down, held_ref, hold, sem):
    del held_ref
    rows = size * UNIT
    copies = [
        pltpu.make_async_copy(c, hold.at[pl.ds((2 * d + 1) * stretch * UNIT + number * rows, rows)], sem.at[d])
        for d, c in enumerate((came_up, came_down))
    ]
    for c in copies:
        c.start()
    for c in copies:
        c.wait()


def couple_kernel(width, depth, many, low, high, begun, threads, loc_ref, when_ref, count_ref, target_ref, coef_ref, metric_ref, *refs):
    refs = list(refs)
    tasks = loc_ref.shape[0] - 1
    acc_ref = refs.pop(0) if begun else None
    line, slots, sems = refs[-3:]
    out_ref = refs[-5] if threads else refs[-4]
    buffers = refs[: -5 if threads else -4]
    out_ref[...] = acc_ref[...] if begun else jnp.zeros_like(out_ref)

    def gather(t, found):
        line[found] = t
        return found + ((when_ref[t] > low) & (when_ref[t] <= high)).astype(jnp.int32)

    found = lax.fori_loop(0, tasks, gather, jnp.int32(0))
    for u in range(many):
        line[found + u] = tasks
    groups = lax.div(found + (many - 1), jnp.int32(many))

    def fetch(group, phase):
        for u in range(many):
            code = loc_ref[line[group * many + u]]
            row = pl.multiple_of(code & ((1 << ROW_BITS) - 1), UNIT)
            for b, source in enumerate(buffers):

                @pl.when((code >> ROW_BITS) == b)
                def _():
                    pltpu.make_async_copy(source.at[pl.ds(row, width)], slots.at[phase, u], sems.at[phase, u]).start()

    @pl.when(groups > 0)
    def _():
        fetch(0, 0)

    @pl.loop(0, groups)
    def _(group):
        phase = lax.rem(group, 2)

        @pl.when(group + 1 < groups)
        def _():
            fetch(group + 1, 1 - phase)

        for u in range(many):
            pltpu.make_async_copy(buffers[0].at[pl.ds(0, width)], slots.at[phase, u], sems.at[phase, u]).wait()
        crossed, amps = [], []
        for u in range(many):
            t = line[group * many + u]
            live = lax.broadcasted_iota(jnp.int32, (width, width), 0) < count_ref[t]
            turned = lax.dot_general(
                slots[phase, u, :, pl.ds(0, depth)],
                metric_ref[target_ref[t]],
                (((1,), (1,)), ((), ())),
                preferred_element_type=jnp.float32,
            )
            crossed.append(jnp.where(live, turned, 0.0).astype(jnp.bfloat16))
            amp = slots[phase, u, :, pl.ds(depth, width)]
            amps.append(jnp.where(live, amp, jnp.zeros_like(amp)))
        halves = [
            lax.dot_general(turned, amp, (((0,), (0,)), ((), ())), preferred_element_type=jnp.float32).astype(jnp.bfloat16)
            for turned, amp in zip(crossed, amps)
        ]
        terms = [
            coef_ref[line[group * many + u]] * jnp.dot(halves[u], crossed[u], preferred_element_type=jnp.float32)
            for u in range(many)
        ]
        for u in range(many):
            target = target_ref[line[group * many + u]]
            out_ref[target] = out_ref[target] - terms[u]


def couple(lists, metric, acc, buffers, low, high, threaded=None):
    tasks, (pairs, width, depth) = lists[0].shape[0] - 1, metric.shape
    many = MANY
    operands = list(lists) + [metric] + ([] if acc is None else [acc]) + buffers
    out_shape = [jax.ShapeDtypeStruct((pairs, width, width), jnp.float32)]
    out_specs, aliases = [IN_VMEM], {}
    if threaded is not None:
        at = len(operands) - len(buffers) + threaded
        aliases = {at: 1}
        out_shape.append(jax.ShapeDtypeStruct(operands[at].shape, operands[at].dtype))
        out_specs.append(ANY)
    return pl.pallas_call(
        functools.partial(couple_kernel, width, depth, many, low, high, acc is not None, threaded is not None),
        in_specs=[SMEM] * 5 + [IN_VMEM] * (1 if acc is None else 2) + [ANY] * len(buffers),
        out_specs=out_specs,
        out_shape=out_shape,
        input_output_aliases=aliases,
        scratch_shapes=[
            pltpu.SMEM((tasks + many,), jnp.int32),
            pltpu.VMEM((2, many, width, depth + width), jnp.bfloat16),
            pltpu.SemaphoreType.DMA((2, many)),
        ],
        compiler_params=params(),
        cost_estimate=pl.CostEstimate(flops=0, bytes_accessed=20_000_000, transcendentals=0),
    )(*operands)


def relay(rounds, size, chips, pairs, width, table, place, need, core, lists, mine, other, metric_of, cross_take, crossed):
    columns = mine.shape[1]
    stretch = rounds * size + 8
    parts = (2, 4, rounds - 3, rounds - 2)
    own = chips - 1
    piece = jax.ShapeDtypeStruct((size * UNIT, columns), mine.dtype)
    double = jax.ShapeDtypeStruct((2 * size * UNIT, columns), mine.dtype)
    stream_shape = jax.ShapeDtypeStruct((2 * rounds * size * UNIT, columns), mine.dtype)
    hold_shape = jax.ShapeDtypeStruct((4 * stretch * UNIT, columns), mine.dtype)
    members = 2 * chips
    ways = [
        [(i, i + 2) for i in range(members - 2)],
        [(i + 2, i) for i in range(members - 2)],
    ]
    across = [(i, i ^ 1) for i in range(members)]
    stream, *opened = pl.pallas_call(
        functools.partial(open_kernel, size, rounds * size, pairs, width, own),
        in_specs=[SMEM] * 4 + [ANY] * 2,
        out_specs=[ANY] + [IN_VMEM] * 2,
        out_shape=[stream_shape] + [double] * 2,
        scratch_shapes=[pltpu.VMEM(mine.shape, mine.dtype)] * 2 + [pltpu.SemaphoreType.DMA] * 2,
        compiler_params=params(),
        cost_estimate=pl.CostEstimate(flops=0, bytes_accessed=6 * mine.size * 2, transcendentals=0),
    )(place, need, table, core, mine, other)
    sends = {1: opened}
    stream, after = lax.optimization_barrier((stream, mine))
    taken = cross_take(after)
    metric, crossing = metric_of(after), crossed(taken)
    hold, swapped, acc, done = None, None, None, -1
    for number in range(1, rounds):
        came = [lax.ppermute(sends[number][d], "mem", ways[d]) for d in range(2)]
        if number == 1:
            *came, _, metric = lax.optimization_barrier((*came, taken, metric))
        else:
            *came, hold = lax.optimization_barrier((*came, hold))
        swapping = [lax.ppermute(came[d], "mem", across) for d in range(2)]
        if number == rounds - 3:
            *came, crossing = lax.optimization_barrier((*came, crossing))
        begun = hold is not None
        ahead = [w for w in ((2, 3) if number == 1 else (number + 2,)) if w < rounds]
        operands = [table, stream] + ([hold] if begun else []) + came + (swapped if begun else [])
        hold, *going = pl.pallas_call(
            functools.partial(
                step_kernel,
                size,
                stretch,
                own,
                0 if number == 1 else number,
                None if not begun else (0 if number == 2 else number - 1),
                ahead,
            ),
            in_specs=[SMEM, ANY] + ([ANY] if begun else []) + [IN_VMEM] * (4 if begun else 2),
            out_specs=[ANY] + [IN_VMEM] * (2 * len(ahead)),
            out_shape=[hold_shape] + [piece] * (2 * len(ahead)),
            input_output_aliases={2: 0} if begun else {},
            scratch_shapes=[pltpu.SemaphoreType.DMA((2,)), pltpu.SemaphoreType.DMA((2,)), pltpu.SemaphoreType.DMA],
            compiler_params=params(),
            cost_estimate=pl.CostEstimate(flops=0, bytes_accessed=12 * size * UNIT * columns * 2, transcendentals=0),
        )(*operands)
        swapped = swapping
        if number in parts:
            buffers = [mine, other, hold] + ([crossing] if number >= rounds - 3 else [])
            acc, hold = couple(lists, metric, acc, buffers, done, number, 2)
            done = number
        for i, window in enumerate(ahead):
            sends[window] = going[2 * i : 2 * i + 2]
    hold = pl.pallas_call(
        functools.partial(close_kernel, size, stretch, rounds - 1),
        in_specs=[IN_VMEM] * 2 + [ANY],
        out_specs=ANY,
        out_shape=hold_shape,
        input_output_aliases={2: 0},
        scratch_shapes=[pltpu.SemaphoreType.DMA((2,))],
        compiler_params=params(),
    )(*swapped, hold)
    [acc] = couple(lists, metric, acc, [mine, other, hold, crossing], done, rounds)
    return acc


def shards(
    pno,
    amplitudes,
    pno_count,
    pao_coupling,
    row_owner,
    row_pair,
    row_target,
    row_coef,
    column_owner,
    column_pair,
    column_target,
    column_coef,
):
    pairs, depth, width = pno.shape
    tasks, crossings = row_pair.shape[0], column_pair.shape[0]
    members, groups = lax.axis_size("mem"), lax.axis_size("grp")
    member, group = lax.axis_index("mem"), lax.axis_index("grp")
    row_cap = max(2, 2 * tasks // members)
    col_cap = max(2, 2 * crossings // groups)
    chips = members // 2
    row_owner, column_owner = row_owner[:, 0], column_owner[:, 0]
    row_code = row_owner * pairs + row_pair
    col_code = column_owner * pairs + column_pair
    tell = jnp.concatenate([row_code, col_code, pno_count])
    told = lax.all_to_all(
        jnp.broadcast_to(tell, (groups * members, tell.shape[0])), ("grp", "mem"), split_axis=0, concat_axis=0, tiled=True
    )
    told = told.reshape(groups, members, -1)
    code, cols, count = told[..., :tasks], told[..., tasks : tasks + crossings], told[..., tasks + crossings :]
    blocks = blocks_of(pno, amplitudes, pno_count)
    ids = jnp.arange(members * pairs, dtype=jnp.int32)
    here = pick(count, group).reshape(-1)
    row_count = jnp.sum(jnp.where(row_code[:, None] == ids, here, 0), axis=1)
    beside = lax.dynamic_index_in_dim(count, member, 1, keepdims=False).reshape(-1)
    col_ids = jnp.arange(groups * pairs, dtype=jnp.int32)
    col_count = jnp.sum(jnp.where(col_code[:, None] == col_ids, beside, 0), axis=1)
    ask = lax.dynamic_index_in_dim(cols, member, 1, keepdims=False)
    asked = wanted_from(ask // pairs, ask % pairs, group, col_cap)
    col_row = (column_owner * col_cap + ranks_of(column_owner)) * width

    def metric_of(blocks):
        return metric_blocks(blocks, pao_coupling).reshape(pairs, width, depth)

    def cross_take(blocks):
        return take(blocks, asked.reshape(-1), width, 1)[0]

    def crossed(sent):
        return lax.all_to_all(sent, "grp", split_axis=0, concat_axis=0, tiled=True)

    def lists_of(location, when, first):
        col_location = col_row + (first << ROW_BITS)
        none = jnp.zeros((1,), jnp.int32)
        return (
            jnp.concatenate([location, col_location, none]),
            jnp.concatenate([when, jnp.full_like(col_location, CROSS_AFTER), none]),
            jnp.concatenate([row_count, col_count, none]),
            jnp.concatenate([row_target, column_target, none]),
            jnp.concatenate([row_coef, column_coef, none.astype(jnp.float32)]),
        )

    def plain(*_):
        want = wanted_from(pick(code, group) // pairs, pick(code, group) % pairs, member, row_cap)
        [sent] = take(blocks, want.reshape(-1), width, 1)
        got = lax.all_to_all(sent, "mem", split_axis=0, concat_axis=0, tiled=True)
        location = (row_owner * row_cap + ranks_of(row_owner)) * width + (1 << ROW_BITS)
        lists = lists_of(location, jnp.zeros_like(location), 2)
        [acc] = couple(lists, metric_of(blocks), None, [blocks, got, crossed(cross_take(blocks))], -1, CROSS_AFTER)
        return acc

    if members % 2 or chips < 2 or chips > 4:
        return plain()
    other = lax.ppermute(blocks, "mem", [(i, i ^ 1) for i in range(members)])
    branch, table, place, need, location, when = relay_plan(code, count, group, member, (row_code, width))
    core = (member % 2).reshape(1).astype(jnp.int32)

    lists = lists_of(location, when, 3)

    def relayed(rounds, size):
        return relay(rounds, size, chips, pairs, width, table, place, need, core, lists, blocks, other, metric_of, cross_take, crossed)

    return lax.switch(branch, [functools.partial(relayed, *p) for p in PLANS] + [plain])


def solution(mesh):
    in_specs = (
        P(("grp", "mem"), None, None),
        P(("grp", "mem"), None, None),
        P(("grp", "mem")),
        P(),
        P(("grp", "mem"), None),
        P(("grp", "mem")),
        P(("grp", "mem")),
        P(("grp", "mem")),
        P(("grp", "mem"), None),
        P(("grp", "mem")),
        P(("grp", "mem")),
        P(("grp", "mem")),
    )
    out_specs = P(("grp", "mem"), None, None)
    return jax.shard_map(shards, mesh=mesh, in_specs=in_specs, out_specs=out_specs, check_vma=False)
```

profile of v0, /device:TPU:0, one launch (start us, length us, event | category | flops | bytes accessed | tf_op | source)
XLA Modules:
  0.0 238.4 jit_solution(911498946592787612)
XLA Ops:
  4.2 7.3 %all-to-all-start.5 = ((s32[32,1,112]{2,1,0:T(1,128)}), s32[32,1,112]{2,1,0:T(1,128)S(1)}, u32[]{:S(2)}, u32[]{:S(2)}) async-start(s32[32,1,112]{2,1,0:T(1,128)} %broadcast_in_dim.217), calls=%async_computation.5 | async-start | bytes 32768 | tf_op jit(solution)/shard_map/all_to_all | solution.py:557
  11.6 7.7 %shard_map.122 = bf16[4096,640]{1,0:T(8,128)(2,1)} custom-call(s32[32]{0:T(128)} %count_ref.1, bf16[32,512,128]{2,1,0:T(8,128)(2,1)} %pno_ref.1, bf16[32,128,128]{2,1,0:T(8,128)(2,1)} %amp_ref.1), custom_call_target="tpu_custom_call" | custom-call | tf_op jit(solution)/shard_map/pallas_call | solution.py:43
  33.9 204.2 %conditional.1 = (f32[32,128,128]{2,1,0:T(8,128)}) conditional(s32[]{:T(128)} %clamp.3, (s32[]{:T(128)}, s32[2,64]{1,0:T(2,128)S(1)}, s32[2,64]{1,0:T(2,128)S(1)}, s32[2,5,3]{1,0,2:T(2,128)S(1)}, bf16[4096,640]{1,0:T(8,128)(2,1)}, /*index=5*/bf16[4096,640]{1,0:T(8,128)(2,1)}, s32[4,8]{1,0:T(4,128)S(1)}, ...), branch_computations={%region_20.21_spmd, %region_21.22_spmd, %region_22.23_spmd, %regio... | conditional | flops 194267 | bytes 418191968 | solution.py:613
  43.9 9.1 %branch_2_fun.17 = (bf16[10368,640]{1,0:T(8,128)(2,1)}, bf16[1152,640]{1,0:T(8,128)(2,1)}, bf16[1152,640]{1,0:T(8,128)(2,1)}) custom-call(s32[2,64]{1,0:T(2,128)S(1)} %get-tuple-element.260.place_ref, s32[2,64]{1,0:T(2,128)S(1)} %get-tuple-element.261.need_ref, s32[2,5,3]{2,1,0:T(8,128)S(1)} %copy.235.runs_ref, s32[1]{0:T(128)} %bitcast.8.core_ref, ...), custom_call_target="tpu_custom_call" | custom-call | bytes 31457280 | tf_op jit(solution)/shard_map/cond/branch_2_fun/pallas_call | solution.py:468
  53.0 4.6 %collective-permute-start.56 = (bf16[1152,640]{1,0:T(8,128)(2,1)}, bf16[1152,640]{1,0:T(8,128)(2,1)S(1)}, u32[]{:S(2)}, u32[]{:S(2)}) collective-permute-start(bf16[1152,640]{1,0:T(8,128)(2,1)} %get-tuple-element.266), channel_id=1, source_target_pairs={{0,2},{1,3},{2,4},{3,5},{4,6},{5,7},{8,10},{9,11},{10,12},{11,13},... | collective-permute-start | bytes 4423688 | tf_op jit(solution)/shard_map/cond/branch_2_fun/ppermute | solution.py:483
  59.0 10.2 %branch_2_fun.18 = bf16[4096,640]{1,0:T(8,128)(2,1)S(1)} custom-call(s32[32]{0:T(128)S(1)} %reshape.710.index_ref, bf16[4096,640]{1,0:T(8,128)(2,1)} %get-tuple-element.270.mine_ref.blocks_ref.block_ref.refs_0_.refs_1_), custom_call_target="tpu_custom_call" | custom-call | bytes 10485760 | tf_op jit(solution)/shard_map/cond/branch_2_fun/pallas_call | solution.py:229
  71.6 5.2 %all-to-all-start.2 = ((bf16[4,1024,640]{2,1,0:T(8,128)(2,1)}), bf16[4,1024,640]{2,1,0:T(8,128)(2,1)}, u32[]{:S(2)}, u32[]{:S(2)}) async-start(bf16[4,1024,640]{2,1,0:T(8,128)(2,1)} %bitcast.334), calls=%async_computation.2 | async-start | bytes 10485760 | tf_op jit(solution)/shard_map/cond/branch_2_fun/all_to_all | solution.py:580
  76.8 6.7 %branch_2_fun.19 = bf16[4096,512]{1,0:T(8,128)(2,1)S(1)} custom-call(bf16[4096,640]{1,0:T(8,128)(2,1)} %get-tuple-element.270.mine_ref.blocks_ref.block_ref.refs_0_.refs_1_, bf16[512,512]{1,0:T(8,128)(2,1)S(1)} %copy-done.17), custom_call_target="tpu_custom_call" | custom-call | bytes 20000000 | tf_op jit(solution)/shard_map/cond/branch_2_fun/pallas_call | solution.py:67
  85.6 4.4 %collective-permute-done.56.refs_0_ = bf16[1152,640]{1,0:T(8,128)(2,1)S(1)} collective-permute-done((bf16[1152,640]{1,0:T(8,128)(2,1)}, bf16[1152,640]{1,0:T(8,128)(2,1)S(1)}, u32[]{:S(2)}, u32[]{:S(2)}) %collective-permute-start.56) | collective-permute-done | bytes 1474592 | tf_op jit(solution)/shard_map/cond/branch_2_fun/ppermute | solution.py:483
  90.0 4.2 %collective-permute-done.57.refs_1_ = bf16[1152,640]{1,0:T(8,128)(2,1)S(1)} collective-permute-done((bf16[1152,640]{1,0:T(8,128)(2,1)}, bf16[1152,640]{1,0:T(8,128)(2,1)S(1)}, u32[]{:S(2)}, u32[]{:S(2)}) %collective-permute-start.57) | collective-permute-done | bytes 1474592 | tf_op jit(solution)/shard_map/cond/branch_2_fun/ppermute | solution.py:483
  97.1 5.3 %collective-permute-start.58 = (bf16[576,640]{1,0:T(8,128)(2,1)S(1)}, bf16[576,640]{1,0:T(8,128)(2,1)S(1)}, u32[]{:S(2)}, u32[]{:S(2)}) collective-permute-start(bf16[576,640]{1,0:T(8,128)(2,1)S(1)} %get-tuple-element.276), channel_id=1, source_target_pairs={{0,2},{1,3},{2,4},{3,5},{4,6},{5,7},{8,10},{9,11},{10,12},{11,13},... | collective-permute-start | bytes 2211848 | tf_op jit(solution)/shard_map/cond/branch_2_fun/ppermute | solution.py:483
  103.7 4.6 %collective-permute-start.64 = (bf16[576,640]{1,0:T(8,128)(2,1)S(1)}, bf16[576,640]{1,0:T(8,128)(2,1)S(1)}, u32[]{:S(2)}, u32[]{:S(2)}) collective-permute-start(bf16[576,640]{1,0:T(8,128)(2,1)S(1)} %get-tuple-element.286), channel_id=1, source_target_pairs={{0,2},{1,3},{2,4},{3,5},{4,6},{5,7},{8,10},{9,11},{10,12},{11,13},... | collective-permute-start | bytes 2211848 | tf_op jit(solution)/shard_map/cond/branch_2_fun/ppermute | solution.py:483
  108.3 10.9 %collective-permute-done.58.refs_1_ = bf16[576,640]{1,0:T(8,128)(2,1)S(1)} collective-permute-done((bf16[576,640]{1,0:T(8,128)(2,1)S(1)}, bf16[576,640]{1,0:T(8,128)(2,1)S(1)}, u32[]{:S(2)}, u32[]{:S(2)}) %collective-permute-start.58) | collective-permute-done | bytes 737312 | tf_op jit(solution)/shard_map/cond/branch_2_fun/ppermute | solution.py:483
  129.8 5.2 %collective-permute-done.64.refs_1_ = bf16[576,640]{1,0:T(8,128)(2,1)S(1)} collective-permute-done((bf16[576,640]{1,0:T(8,128)(2,1)S(1)}, bf16[576,640]{1,0:T(8,128)(2,1)S(1)}, u32[]{:S(2)}, u32[]{:S(2)}) %collective-permute-start.64) | collective-permute-done | bytes 737312 | tf_op jit(solution)/shard_map/cond/branch_2_fun/ppermute | solution.py:483
  136.3 7.4 %branch_2_fun.22 = (f32[32,128,128]{2,1,0:T(8,128)S(1)}, bf16[21248,640]{1,0:T(8,128)(2,1)}) custom-call(s32[81]{0:T(128)S(1)} %get-tuple-element.255.loc_ref, s32[81]{0:T(128)S(1)} %copy-done.21, s32[81]{0:T(128)S(1)} %get-tuple-element.257.count_ref, s32[81]{0:T(128)S(1)} %get-tuple-element.258.target_ref, ...), custom_call_target="tpu_custom_call", output_to_operand_aliasing={{1}: (8, {})} | custom-call | bytes 20000000 | tf_op jit(solution)/shard_map/cond/branch_2_fun/pallas_call | solution.py:437
  146.7 9.0 %collective-permute-start.72 = (bf16[576,640]{1,0:T(8,128)(2,1)S(1)}, bf16[576,640]{1,0:T(8,128)(2,1)}, u32[]{:S(2)}, u32[]{:S(2)}) collective-permute-start(bf16[576,640]{1,0:T(8,128)(2,1)S(1)} %get-tuple-element.300), channel_id=1, source_target_pairs={{0,2},{1,3},{2,4},{3,5},{4,6},{5,7},{8,10},{9,11},{10,12},{11,13},... | collective-permute-start | bytes 2211848 | tf_op jit(solution)/shard_map/cond/branch_2_fun/ppermute | solution.py:483
  159.9 5.2 %collective-permute-start.70 = (bf16[576,640]{1,0:T(8,128)(2,1)S(1)}, bf16[576,640]{1,0:T(8,128)(2,1)S(1)}, u32[]{:S(2)}, u32[]{:S(2)}) collective-permute-start(bf16[576,640]{1,0:T(8,128)(2,1)S(1)} %get-tuple-element.298), channel_id=1, source_target_pairs={{0,2},{1,3},{2,4},{3,5},{4,6},{5,7},{8,10},{9,11},{10,12},{11,13},... | collective-permute-start | bytes 2211848 | tf_op jit(solution)/shard_map/cond/branch_2_fun/ppermute | solution.py:483
  165.1 6.5 %collective-permute-done.72.refs_1_ = bf16[576,640]{1,0:T(8,128)(2,1)} collective-permute-done((bf16[576,640]{1,0:T(8,128)(2,1)S(1)}, bf16[576,640]{1,0:T(8,128)(2,1)}, u32[]{:S(2)}, u32[]{:S(2)}) %collective-permute-start.72) | collective-permute-done | bytes 737312 | tf_op jit(solution)/shard_map/cond/branch_2_fun/ppermute | solution.py:483
  172.9 7.6 %branch_2_fun.25 = (f32[32,128,128]{2,1,0:T(8,128)S(1)}, bf16[21248,640]{1,0:T(8,128)(2,1)}) custom-call(s32[81]{0:T(128)S(1)} %get-tuple-element.255.loc_ref, s32[81]{0:T(128)S(1)} %copy-done.21, s32[81]{0:T(128)S(1)} %get-tuple-element.257.count_ref, s32[81]{0:T(128)S(1)} %get-tuple-element.258.target_ref, ...), custom_call_target="tpu_custom_call", output_to_operand_aliasing={{1}: (9, {})} | custom-call | bytes 20000000 | tf_op jit(solution)/shard_map/cond/branch_2_fun/pallas_call | solution.py:437
  185.2 4.3 %collective-permute-start.78 = (bf16[576,640]{1,0:T(8,128)(2,1)}, bf16[576,640]{1,0:T(8,128)(2,1)}, u32[]{:S(2)}, u32[]{:S(2)}) collective-permute-start(bf16[576,640]{1,0:T(8,128)(2,1)} %get-tuple-element.315), channel_id=1, source_target_pairs={{0,2},{1,3},{2,4},{3,5},{4,6},{5,7},{8,10},{9,11},{10,12},{11,13},... | collective-permute-start | bytes 2211848 | tf_op jit(solution)/shard_map/cond/branch_2_fun/ppermute | solution.py:483
  198.5 4.6 %collective-permute-start.82 = (bf16[576,640]{1,0:T(8,128)(2,1)S(1)}, bf16[576,640]{1,0:T(8,128)(2,1)S(1)}, u32[]{:S(2)}, u32[]{:S(2)}) collective-permute-start(bf16[576,640]{1,0:T(8,128)(2,1)S(1)} %get-tuple-element.322), channel_id=1, source_target_pairs={{0,2},{1,3},{2,4},{3,5},{4,6},{5,7},{8,10},{9,11},{10,12},{11,13},... | collective-permute-start | bytes 2211848 | tf_op jit(solution)/shard_map/cond/branch_2_fun/ppermute | solution.py:483
  207.1 8.2 %branch_2_fun.28 = (f32[32,128,128]{2,1,0:T(8,128)S(1)}, bf16[21248,640]{1,0:T(8,128)(2,1)}) custom-call(s32[81]{0:T(128)S(1)} %get-tuple-element.255.loc_ref, s32[81]{0:T(128)S(1)} %copy-done.21, s32[81]{0:T(128)S(1)} %get-tuple-element.257.count_ref, s32[81]{0:T(128)S(1)} %get-tuple-element.258.target_ref, ...), custom_call_target="tpu_custom_call", output_to_operand_aliasing={{1}: (9, {})} | custom-call | bytes 20000000 | tf_op jit(solution)/shard_map/cond/branch_2_fun/pallas_call | solution.py:437
  219.2 6.1 %branch_2_fun.30 = (f32[32,128,128]{2,1,0:T(8,128)S(1)}, bf16[21248,640]{1,0:T(8,128)(2,1)}) custom-call(s32[81]{0:T(128)S(1)} %get-tuple-element.255.loc_ref, s32[81]{0:T(128)S(1)} %copy-done.21, s32[81]{0:T(128)S(1)} %get-tuple-element.257.count_ref, s32[81]{0:T(128)S(1)} %get-tuple-element.258.target_ref, ...), custom_call_target="tpu_custom_call", output_to_operand_aliasing={{1}: (9, {})} | custom-call | bytes 20000000 | tf_op jit(solution)/shard_map/cond/branch_2_fun/pallas_call | solution.py:437
  231.4 6.8 %branch_2_fun.33 = f32[32,128,128]{2,1,0:T(8,128)} custom-call(s32[81]{0:T(128)S(1)} %get-tuple-element.255.loc_ref, s32[81]{0:T(128)S(1)} %copy-done.21, s32[81]{0:T(128)S(1)} %get-tuple-element.257.count_ref, s32[81]{0:T(128)S(1)} %get-tuple-element.258.target_ref, f32[81]{0:T(128)S(1)} %get-tuple-element.259.coef_ref, bf16[32,128,512]{2,1,0:T(8,128)(2,1)} %bitcast.323, ...), custom_call_target="tpu_custom_call" | custom-call | bytes 20000000 | tf_op jit(solution)/shard_map/cond/branch_2_fun/pallas_call | solution.py:437
  (235 shorter events, 74.8 us)
Async XLA Ops:
  53.0 37.0 %collective-permute-start.56 = (bf16[1152,640]{1,0:T(8,128)(2,1)}, bf16[1152,640]{1,0:T(8,128)(2,1)S(1)}, u32[]{:S(2)}, u32[]{:S(2)}) collective-permute-start(bf16[1152,640]{1,0:T(8,128)(2,1)} %get-tuple-element.266), channel_id=1, source_target_pairs={{0,2},{1,3},{2,4},{3,5},{4,6},{5,7},{8,10},{9,11},{10,12},{11,13},... | collective-permute-start | bytes 4423688 | tf_op jit(solution)/shard_map/cond/branch_2_fun/ppermute | solution.py:483
  57.6 36.6 %collective-permute-start.57 = (bf16[1152,640]{1,0:T(8,128)(2,1)}, bf16[1152,640]{1,0:T(8,128)(2,1)S(1)}, u32[]{:S(2)}, u32[]{:S(2)}) collective-permute-start(bf16[1152,640]{1,0:T(8,128)(2,1)} %get-tuple-element.267), channel_id=1, source_target_pairs={{2,0},{3,1},{4,2},{5,3},{6,4},{7,5},{10,8},{11,9},{12,10},{13,11},... | collective-permute-start | bytes 4423688 | tf_op jit(solution)/shard_map/cond/branch_2_fun/ppermute | solution.py:483
  71.6 122.2 %all-to-all-start.2 = ((bf16[4,1024,640]{2,1,0:T(8,128)(2,1)}), bf16[4,1024,640]{2,1,0:T(8,128)(2,1)}, u32[]{:S(2)}, u32[]{:S(2)}) async-start(bf16[4,1024,640]{2,1,0:T(8,128)(2,1)} %bitcast.334), calls=%async_computation.2 | async-start | bytes 10485760 | tf_op jit(solution)/shard_map/cond/branch_2_fun/all_to_all | solution.py:580
  94.2 28.2 %collective-permute-start.60 = (bf16[1152,640]{1,0:T(8,128)(2,1)S(1)}, bf16[1152,640]{1,0:T(8,128)(2,1)S(1)}, u32[]{:S(2)}, u32[]{:S(2)}) collective-permute-start(bf16[1152,640]{1,0:T(8,128)(2,1)S(1)} %collective-permute-done.56.refs_0_), channel_id=1, source_target_pairs={{0,1},{1,0},{2,3},{3,2},{4,5},{5,4},{6,7},{7,6},{8,9},{9,8},{10,11... | collective-permute-start | bytes 4423688 | tf_op jit(solution)/shard_map/cond/branch_2_fun/ppermute | solution.py:488
  94.2 28.7 %collective-permute-start.61 = (bf16[1152,640]{1,0:T(8,128)(2,1)S(1)}, bf16[1152,640]{1,0:T(8,128)(2,1)S(1)}, u32[]{:S(2)}, u32[]{:S(2)}) collective-permute-start(bf16[1152,640]{1,0:T(8,128)(2,1)S(1)} %collective-permute-done.57.refs_1_), channel_id=1, source_target_pairs={{0,1},{1,0},{2,3},{3,2},{4,5},{5,4},{6,7},{7,6},{8,9},{9,8},{10,11... | collective-permute-start | bytes 4423688 | tf_op jit(solution)/shard_map/cond/branch_2_fun/ppermute | solution.py:488
  97.1 22.1 %collective-permute-start.58 = (bf16[576,640]{1,0:T(8,128)(2,1)S(1)}, bf16[576,640]{1,0:T(8,128)(2,1)S(1)}, u32[]{:S(2)}, u32[]{:S(2)}) collective-permute-start(bf16[576,640]{1,0:T(8,128)(2,1)S(1)} %get-tuple-element.276), channel_id=1, source_target_pairs={{0,2},{1,3},{2,4},{3,5},{4,6},{5,7},{8,10},{9,11},{10,12},{11,13},... | collective-permute-start | bytes 2211848 | tf_op jit(solution)/shard_map/cond/branch_2_fun/ppermute | solution.py:483
  102.4 20.0 %collective-permute-start.59 = (bf16[576,640]{1,0:T(8,128)(2,1)S(1)}, bf16[576,640]{1,0:T(8,128)(2,1)S(1)}, u32[]{:S(2)}, u32[]{:S(2)}) collective-permute-start(bf16[576,640]{1,0:T(8,128)(2,1)S(1)} %get-tuple-element.277), channel_id=1, source_target_pairs={{2,0},{3,1},{4,2},{5,3},{6,4},{7,5},{10,8},{11,9},{12,10},{13,11},... | collective-permute-start | bytes 2211848 | tf_op jit(solution)/shard_map/cond/branch_2_fun/ppermute | solution.py:483
  103.7 31.3 %collective-permute-start.64 = (bf16[576,640]{1,0:T(8,128)(2,1)S(1)}, bf16[576,640]{1,0:T(8,128)(2,1)S(1)}, u32[]{:S(2)}, u32[]{:S(2)}) collective-permute-start(bf16[576,640]{1,0:T(8,128)(2,1)S(1)} %get-tuple-element.286), channel_id=1, source_target_pairs={{0,2},{1,3},{2,4},{3,5},{4,6},{5,7},{8,10},{9,11},{10,12},{11,13},... | collective-permute-start | bytes 2211848 | tf_op jit(solution)/shard_map/cond/branch_2_fun/ppermute | solution.py:483
  119.2 24.5 %collective-permute-start.65 = (bf16[576,640]{1,0:T(8,128)(2,1)S(1)}, bf16[576,640]{1,0:T(8,128)(2,1)S(1)}, u32[]{:S(2)}, u32[]{:S(2)}) collective-permute-start(bf16[576,640]{1,0:T(8,128)(2,1)S(1)} %get-tuple-element.287), channel_id=1, source_target_pairs={{2,0},{3,1},{4,2},{5,3},{6,4},{7,5},{10,8},{11,9},{12,10},{13,11},... | collective-permute-start | bytes 2211848 | tf_op jit(solution)/shard_map/cond/branch_2_fun/ppermute | solution.py:483
  122.4 21.4 %collective-permute-start.66 = (bf16[576,640]{1,0:T(8,128)(2,1)S(1)}, bf16[576,640]{1,0:T(8,128)(2,1)S(1)}, u32[]{:S(2)}, u32[]{:S(2)}) collective-permute-start(bf16[576,640]{1,0:T(8,128)(2,1)S(1)} %collective-permute-done.58.refs_1_), channel_id=1, source_target_pairs={{0,1},{1,0},{2,3},{3,2},{4,5},{5,4},{6,7},{7,6},{8,9},{9,8},{10,11... | collective-permute-start | bytes 2211848 | tf_op jit(solution)/shard_map/cond/branch_2_fun/ppermute | solution.py:488
  122.4 21.9 %collective-permute-start.67 = (bf16[576,640]{1,0:T(8,128)(2,1)S(1)}, bf16[576,640]{1,0:T(8,128)(2,1)S(1)}, u32[]{:S(2)}, u32[]{:S(2)}) collective-permute-start(bf16[576,640]{1,0:T(8,128)(2,1)S(1)} %collective-permute-done.59.refs_2_), channel_id=1, source_target_pairs={{0,1},{1,0},{2,3},{3,2},{4,5},{5,4},{6,7},{7,6},{8,9},{9,8},{10,11... | collective-permute-start | bytes 2211848 | tf_op jit(solution)/shard_map/cond/branch_2_fun/ppermute | solution.py:488
  125.7 29.9 %collective-permute-start.62 = (bf16[576,640]{1,0:T(8,128)(2,1)S(1)}, bf16[576,640]{1,0:T(8,128)(2,1)S(1)}, u32[]{:S(2)}, u32[]{:S(2)}) collective-permute-start(bf16[576,640]{1,0:T(8,128)(2,1)S(1)} %get-tuple-element.284), channel_id=1, source_target_pairs={{0,2},{1,3},{2,4},{3,5},{4,6},{5,7},{8,10},{9,11},{10,12},{11,13},... | collective-permute-start | bytes 2211848 | tf_op jit(solution)/shard_map/cond/branch_2_fun/ppermute | solution.py:483
  135.0 21.9 %collective-permute-start.63 = (bf16[576,640]{1,0:T(8,128)(2,1)S(1)}, bf16[576,640]{1,0:T(8,128)(2,1)S(1)}, u32[]{:S(2)}, u32[]{:S(2)}) collective-permute-start(bf16[576,640]{1,0:T(8,128)(2,1)S(1)} %get-tuple-element.285), channel_id=1, source_target_pairs={{2,0},{3,1},{4,2},{5,3},{6,4},{7,5},{10,8},{11,9},{12,10},{13,11},... | collective-permute-start | bytes 2211848 | tf_op jit(solution)/shard_map/cond/branch_2_fun/ppermute | solution.py:483
  146.7 25.0 %collective-permute-start.72 = (bf16[576,640]{1,0:T(8,128)(2,1)S(1)}, bf16[576,640]{1,0:T(8,128)(2,1)}, u32[]{:S(2)}, u32[]{:S(2)}) collective-permute-start(bf16[576,640]{1,0:T(8,128)(2,1)S(1)} %get-tuple-element.300), channel_id=1, source_target_pairs={{0,2},{1,3},{2,4},{3,5},{4,6},{5,7},{8,10},{9,11},{10,12},{11,13},... | collective-permute-start | bytes 2211848 | tf_op jit(solution)/shard_map/cond/branch_2_fun/ppermute | solution.py:483
  155.7 24.8 %collective-permute-start.73 = (bf16[576,640]{1,0:T(8,128)(2,1)S(1)}, bf16[576,640]{1,0:T(8,128)(2,1)}, u32[]{:S(2)}, u32[]{:S(2)}) collective-permute-start(bf16[576,640]{1,0:T(8,128)(2,1)S(1)} %get-tuple-element.301), channel_id=1, source_target_pairs={{2,0},{3,1},{4,2},{5,3},{6,4},{7,5},{10,8},{11,9},{12,10},{13,11},... | collective-permute-start | bytes 2211848 | tf_op jit(solution)/shard_map/cond/branch_2_fun/ppermute | solution.py:483
  157.0 23.6 %collective-permute-start.74 = (bf16[576,640]{1,0:T(8,128)(2,1)S(1)}, bf16[576,640]{1,0:T(8,128)(2,1)S(1)}, u32[]{:S(2)}, u32[]{:S(2)}) collective-permute-start(bf16[576,640]{1,0:T(8,128)(2,1)S(1)} %collective-permute-done.62.refs_1_), channel_id=1, source_target_pairs={{0,1},{1,0},{2,3},{3,2},{4,5},{5,4},{6,7},{7,6},{8,9},{9,8},{10,11... | collective-permute-start | bytes 2211848 | tf_op jit(solution)/shard_map/cond/branch_2_fun/ppermute | solution.py:488
  157.1 24.0 %collective-permute-start.75 = (bf16[576,640]{1,0:T(8,128)(2,1)S(1)}, bf16[576,640]{1,0:T(8,128)(2,1)S(1)}, u32[]{:S(2)}, u32[]{:S(2)}) collective-permute-start(bf16[576,640]{1,0:T(8,128)(2,1)S(1)} %collective-permute-done.63.refs_2_), channel_id=1, source_target_pairs={{0,1},{1,0},{2,3},{3,2},{4,5},{5,4},{6,7},{7,6},{8,9},{9,8},{10,11... | collective-permute-start | bytes 2211848 | tf_op jit(solution)/shard_map/cond/branch_2_fun/ppermute | solution.py:488
  159.9 29.7 %collective-permute-start.70 = (bf16[576,640]{1,0:T(8,128)(2,1)S(1)}, bf16[576,640]{1,0:T(8,128)(2,1)S(1)}, u32[]{:S(2)}, u32[]{:S(2)}) collective-permute-start(bf16[576,640]{1,0:T(8,128)(2,1)S(1)} %get-tuple-element.298), channel_id=1, source_target_pairs={{0,2},{1,3},{2,4},{3,5},{4,6},{5,7},{8,10},{9,11},{10,12},{11,13},... | collective-permute-start | bytes 2211848 | tf_op jit(solution)/shard_map/cond/branch_2_fun/ppermute | solution.py:483
  185.2 20.6 %collective-permute-start.78 = (bf16[576,640]{1,0:T(8,128)(2,1)}, bf16[576,640]{1,0:T(8,128)(2,1)}, u32[]{:S(2)}, u32[]{:S(2)}) collective-permute-start(bf16[576,640]{1,0:T(8,128)(2,1)} %get-tuple-element.315), channel_id=1, source_target_pairs={{0,2},{1,3},{2,4},{3,5},{4,6},{5,7},{8,10},{9,11},{10,12},{11,13},... | collective-permute-start | bytes 2211848 | tf_op jit(solution)/shard_map/cond/branch_2_fun/ppermute | solution.py:483
  192.4 22.9 %collective-permute-start.79 = (bf16[576,640]{1,0:T(8,128)(2,1)}, bf16[576,640]{1,0:T(8,128)(2,1)}, u32[]{:S(2)}, u32[]{:S(2)}) collective-permute-start(bf16[576,640]{1,0:T(8,128)(2,1)} %get-tuple-element.316), channel_id=1, source_target_pairs={{2,0},{3,1},{4,2},{5,3},{6,4},{7,5},{10,8},{11,9},{12,10},{13,11},... | collective-permute-start | bytes 2211848 | tf_op jit(solution)/shard_map/cond/branch_2_fun/ppermute | solution.py:483
  193.7 21.7 %collective-permute-start.80 = (bf16[576,640]{1,0:T(8,128)(2,1)S(1)}, bf16[576,640]{1,0:T(8,128)(2,1)}, u32[]{:S(2)}, u32[]{:S(2)}) collective-permute-start(bf16[576,640]{1,0:T(8,128)(2,1)S(1)} %collective-permute-done.70.refs_1_), channel_id=1, source_target_pairs={{0,1},{1,0},{2,3},{3,2},{4,5},{5,4},{6,7},{7,6},{8,9},{9,8},{10,11... | collective-permute-start | bytes 2211848 | tf_op jit(solution)/shard_map/cond/branch_2_fun/ppermute | solution.py:488
  193.8 22.1 %collective-permute-start.81 = (bf16[576,640]{1,0:T(8,128)(2,1)}, bf16[576,640]{1,0:T(8,128)(2,1)S(1)}, u32[]{:S(2)}, u32[]{:S(2)}) collective-permute-start(bf16[576,640]{1,0:T(8,128)(2,1)} %copy-done.11), channel_id=1, source_target_pairs={{0,1},{1,0},{2,3},{3,2},{4,5},{5,4},{6,7},{7,6},{8,9},{9,8},{10,11... | collective-permute-start | bytes 2211848 | tf_op jit(solution)/shard_map/cond/branch_2_fun/ppermute | solution.py:488
  198.5 26.8 %collective-permute-start.82 = (bf16[576,640]{1,0:T(8,128)(2,1)S(1)}, bf16[576,640]{1,0:T(8,128)(2,1)S(1)}, u32[]{:S(2)}, u32[]{:S(2)}) collective-permute-start(bf16[576,640]{1,0:T(8,128)(2,1)S(1)} %get-tuple-element.322), channel_id=1, source_target_pairs={{0,2},{1,3},{2,4},{3,5},{4,6},{5,7},{8,10},{9,11},{10,12},{11,13},... | collective-permute-start | bytes 2211848 | tf_op jit(solution)/shard_map/cond/branch_2_fun/ppermute | solution.py:483
  205.8 21.1 %collective-permute-start.83 = (bf16[576,640]{1,0:T(8,128)(2,1)S(1)}, bf16[576,640]{1,0:T(8,128)(2,1)S(1)}, u32[]{:S(2)}, u32[]{:S(2)}) collective-permute-start(bf16[576,640]{1,0:T(8,128)(2,1)S(1)} %get-tuple-element.323), channel_id=1, source_target_pairs={{2,0},{3,1},{4,2},{5,3},{6,4},{7,5},{10,8},{11,9},{12,10},{13,11},... | collective-permute-start | bytes 2211848 | tf_op jit(solution)/shard_map/cond/branch_2_fun/ppermute | solution.py:483
  (25 other events, 232.3 us)
where the time goes:
time: 242 us; the launch traced here: 238 us
  Pallas kernels  93.5 us (39%)
  starting transfers between devices  69 us (29%)
  waiting for transfers between devices  40 us (17%)
  local copies, waits for them, and re-layouts  12.6 us (5%)
  other arithmetic  11 us (5%)
  loops' own time  9.59 us (4%)
  between operations  2.71 us (1%)
    ppermute x16, starting transfers between devices, relay(): came = [lax.ppermute(sends[number][d], 'mem', ways[d]) for d in range(2)]  52 us
    ppermute x16, waiting for transfers between devices, relay(): came = [lax.ppermute(sends[number][d], 'mem', ways[d]) for d in range(2)]  39.5 us
    pallas_call x5, Pallas kernels, couple(): pl.pallas_call(functools.partial(couple_kernel, width, depth, many, low,...  36.1 us
    pallas_call x8, Pallas kernels, relay(): pl.pallas_call(functools.partial(step_kernel, size, stretch, own, 0 if nu...  22.5 us
    pallas_call x1, Pallas kernels, take(): pl.pallas_call(functools.partial(take_kernel, width), in_specs=[SMEM, ANY...  10.2 us
    another operation x1, loops' own time, shards(): lax.switch(branch, [functools.partial(relayed, *p) for p in PLANS] + [pla...  9.59 us
    pallas_call x1, Pallas kernels, relay(): pl.pallas_call(functools.partial(open_kernel, size, rounds * size, pairs,...  9.07 us
    pallas_call x1, Pallas kernels, blocks_of(): pl.pallas_call(block_kernel, grid=(pairs // many,), in_specs=[SMEM, pl.Bl...  7.71 us
  transfers between devices with their start and end apart: 35, of which 10 were waited for; matrix products, arithmetic and copies ran while one was open for 5% of the time, Pallas kernels for 32%

commit v1 on v0

--- a/solution.py
+++ b/solution.py
@@ -8,7 +8,7 @@
 from jax.sharding import PartitionSpec as P
 
 UNIT = 16
-PLANS = ((8, 35), (8, 37), (9, 36))
+PLANS = ((8, 37), (9, 36))
 VMEM = 48 * 2**20
 CROSS_AFTER = 5
 ROW_BITS = 20

time: 242 us -> 225 us (0.930); the launches traced: 238 us -> 225 us
  loops' own time: 9.59 us -> 0.69 us
    another operation x1, loops' own time: 9.59 us -> 0.69 us  [shards(): lax.switch(branch, [functools.partial(relayed, *p) for p in PLANS] + [pla...]
    pallas_call x5, Pallas kernels: 36.1 us -> 33 us  [couple(): pl.pallas_call(functools.partial(couple_kernel, width, depth, many, low,...]
    cond x18 -> x14, local copies, waits for them, and re-layouts: 7.15 us -> 7.4 us
  transfers between devices with their start and end apart: 35 -> 35, of which waited for: 10 -> 9; matrix products, arithmetic and copies ran while one was open for 5% -> 5% of each run, Pallas kernels for 32% -> 34%
where the time goes in v1:
time: 225 us
  Pallas kernels  91.6 us (41%)
  starting transfers between devices  66.7 us (30%)
  waiting for transfers between devices  41.8 us (19%)
  local copies, waits for them, and re-layouts  13 us (6%)
  other arithmetic  9.67 us (4%)
    ppermute x16, starting transfers between devices, relay(): came = [lax.ppermute(sends[number][d], 'mem', ways[d]) for d in range(2)]  49.6 us
    ppermute x16, waiting for transfers between devices, relay(): came = [lax.ppermute(sends[number][d], 'mem', ways[d]) for d in range(2)]  41.4 us
    pallas_call x5, Pallas kernels, couple(): pl.pallas_call(functools.partial(couple_kernel, width, depth, many, low,...  33 us
    pallas_call x8, Pallas kernels, relay(): pl.pallas_call(functools.partial(step_kernel, size, stretch, own, 0 if nu...  23.2 us
    pallas_call x1, Pallas kernels, take(): pl.pallas_call(functools.partial(take_kernel, width), in_specs=[SMEM, ANY...  10.2 us
    pallas_call x1, Pallas kernels, relay(): pl.pallas_call(functools.partial(open_kernel, size, rounds * size, pairs,...  9.62 us
    pallas_call x1, Pallas kernels, blocks_of(): pl.pallas_call(block_kernel, grid=(pairs // many,), in_specs=[SMEM, pl.Bl...  7.62 us
    cond x14, local copies, waits for them, and re-layouts  7.4 us
  transfers between devices with their start and end apart: 35, of which 9 were waited for; matrix products, arithmetic and copies ran while one was open for 5% of the time, Pallas kernels for 34%

profile of v1, /device:TPU:0, one launch (start us, length us, event | category | flops | bytes accessed | tf_op | source)
XLA Modules:
  0.0 225.3 jit_solution(12685279238167917811)
XLA Ops:
  3.6 7.3 %all-to-all-start.4 = ((s32[32,1,112]{2,1,0:T(1,128)}), s32[32,1,112]{2,1,0:T(1,128)S(1)}, u32[]{:S(2)}, u32[]{:S(2)}) async-start(s32[32,1,112]{2,1,0:T(1,128)} %broadcast_in_dim.217), calls=%async_computation.4 | async-start | bytes 32768 | tf_op jit(solution)/shard_map/all_to_all | solution.py:557
  11.0 7.6 %shard_map.121 = bf16[4096,640]{1,0:T(8,128)(2,1)} custom-call(s32[32]{0:T(128)} %count_ref.1, bf16[32,512,128]{2,1,0:T(8,128)(2,1)} %pno_ref.1, bf16[32,128,128]{2,1,0:T(8,128)(2,1)} %amp_ref.1), custom_call_target="tpu_custom_call" | custom-call | tf_op jit(solution)/shard_map/pallas_call | solution.py:43
  32.0 193.2 %conditional.1 = (f32[32,128,128]{2,1,0:T(8,128)}) conditional(s32[]{:T(128)} %clamp.3, (s32[]{:T(128)}, s32[2,64]{1,0:T(2,128)S(1)}, s32[2,64]{1,0:T(2,128)S(1)}, s32[2,5,3]{1,0,2:T(2,128)S(1)}, bf16[4096,640]{1,0:T(8,128)(2,1)}, /*index=5*/bf16[4096,640]{1,0:T(8,128)(2,1)}, s32[4,8]{1,0:T(4,128)S(1)}, ...), branch_computations={%region_19.20_spmd, %region_20.21_spmd, %region_21.25_spmd} | conditional | flops 194267 | bytes 400368928 | solution.py:613
  33.4 9.6 %branch_1_fun.17 = (bf16[10368,640]{1,0:T(8,128)(2,1)}, bf16[1152,640]{1,0:T(8,128)(2,1)}, bf16[1152,640]{1,0:T(8,128)(2,1)}) custom-call(s32[2,64]{1,0:T(2,128)} %copy-done.15, s32[2,64]{1,0:T(2,128)} %copy-done.14, s32[2,5,3]{2,1,0:T(8,128)S(1)} %copy.219.runs_ref, s32[1]{0:T(128)} %bitcast.4.core_ref, ...), custom_call_target="tpu_custom_call" | custom-call | bytes 31457280 | tf_op jit(solution)/shard_map/cond/branch_1_fun/pallas_call | solution.py:468
  48.1 10.2 %branch_1_fun.18 = bf16[4096,640]{1,0:T(8,128)(2,1)S(1)} custom-call(s32[32]{0:T(128)S(1)} %reshape.699.index_ref, bf16[4096,640]{1,0:T(8,128)(2,1)} %get-tuple-element.175.mine_ref.blocks_ref.block_ref.refs_0_.refs_1_), custom_call_target="tpu_custom_call" | custom-call | bytes 10485760 | tf_op jit(solution)/shard_map/cond/branch_1_fun/pallas_call | solution.py:229
  60.7 5.2 %all-to-all-start.1 = ((bf16[4,1024,640]{2,1,0:T(8,128)(2,1)}), bf16[4,1024,640]{2,1,0:T(8,128)(2,1)}, u32[]{:S(2)}, u32[]{:S(2)}) async-start(bf16[4,1024,640]{2,1,0:T(8,128)(2,1)} %bitcast.296), calls=%async_computation.1 | async-start | bytes 10485760 | tf_op jit(solution)/shard_map/cond/branch_1_fun/all_to_all | solution.py:580
  65.9 6.7 %branch_1_fun.19 = bf16[4096,512]{1,0:T(8,128)(2,1)S(1)} custom-call(bf16[4096,640]{1,0:T(8,128)(2,1)} %get-tuple-element.175.mine_ref.blocks_ref.block_ref.refs_0_.refs_1_, bf16[512,512]{1,0:T(8,128)(2,1)S(1)} %copy-done.12), custom_call_target="tpu_custom_call" | custom-call | bytes 20000000 | tf_op jit(solution)/shard_map/cond/branch_1_fun/pallas_call | solution.py:67
  74.6 4.3 %collective-permute-done.28.refs_0_ = bf16[1152,640]{1,0:T(8,128)(2,1)S(1)} collective-permute-done((bf16[1152,640]{1,0:T(8,128)(2,1)}, bf16[1152,640]{1,0:T(8,128)(2,1)S(1)}, u32[]{:S(2)}, u32[]{:S(2)}) %collective-permute-start.28) | collective-permute-done | bytes 1474592 | tf_op jit(solution)/shard_map/cond/branch_1_fun/ppermute | solution.py:483
  79.0 4.1 %collective-permute-done.29.refs_1_ = bf16[1152,640]{1,0:T(8,128)(2,1)S(1)} collective-permute-done((bf16[1152,640]{1,0:T(8,128)(2,1)}, bf16[1152,640]{1,0:T(8,128)(2,1)S(1)}, u32[]{:S(2)}, u32[]{:S(2)}) %collective-permute-start.29) | collective-permute-done | bytes 1474592 | tf_op jit(solution)/shard_map/cond/branch_1_fun/ppermute | solution.py:483
  86.6 4.6 %collective-permute-start.30 = (bf16[576,640]{1,0:T(8,128)(2,1)S(1)}, bf16[576,640]{1,0:T(8,128)(2,1)S(1)}, u32[]{:S(2)}, u32[]{:S(2)}) collective-permute-start(bf16[576,640]{1,0:T(8,128)(2,1)S(1)} %get-tuple-element.181), channel_id=1, source_target_pairs={{0,2},{1,3},{2,4},{3,5},{4,6},{5,7},{8,10},{9,11},{10,12},{11,13},... | collective-permute-start | bytes 2211848 | tf_op jit(solution)/shard_map/cond/branch_1_fun/ppermute | solution.py:483
  92.5 4.6 %collective-permute-start.36 = (bf16[576,640]{1,0:T(8,128)(2,1)S(1)}, bf16[576,640]{1,0:T(8,128)(2,1)S(1)}, u32[]{:S(2)}, u32[]{:S(2)}) collective-permute-start(bf16[576,640]{1,0:T(8,128)(2,1)S(1)} %get-tuple-element.191), channel_id=1, source_target_pairs={{0,2},{1,3},{2,4},{3,5},{4,6},{5,7},{8,10},{9,11},{10,12},{11,13},... | collective-permute-start | bytes 2211848 | tf_op jit(solution)/shard_map/cond/branch_1_fun/ppermute | solution.py:483
  97.1 10.9 %collective-permute-done.30.refs_1_ = bf16[576,640]{1,0:T(8,128)(2,1)S(1)} collective-permute-done((bf16[576,640]{1,0:T(8,128)(2,1)S(1)}, bf16[576,640]{1,0:T(8,128)(2,1)S(1)}, u32[]{:S(2)}, u32[]{:S(2)}) %collective-permute-start.30) | collective-permute-done | bytes 737312 | tf_op jit(solution)/shard_map/cond/branch_1_fun/ppermute | solution.py:483
  118.5 5.3 %collective-permute-done.36.refs_1_ = bf16[576,640]{1,0:T(8,128)(2,1)S(1)} collective-permute-done((bf16[576,640]{1,0:T(8,128)(2,1)S(1)}, bf16[576,640]{1,0:T(8,128)(2,1)S(1)}, u32[]{:S(2)}, u32[]{:S(2)}) %collective-permute-start.36) | collective-permute-done | bytes 737312 | tf_op jit(solution)/shard_map/cond/branch_1_fun/ppermute | solution.py:483
  125.1 10.4 %branch_1_fun.22 = (f32[32,128,128]{2,1,0:T(8,128)S(1)}, bf16[21248,640]{1,0:T(8,128)(2,1)}) custom-call(s32[81]{0:T(128)S(1)} %get-tuple-element.160.loc_ref, s32[81]{0:T(128)S(1)} %get-tuple-element.161.when_ref, s32[81]{0:T(128)S(1)} %get-tuple-element.162.count_ref, s32[81]{0:T(128)S(1)} %get-tuple-element.163.target_ref, ...), custom_call_target="tpu_custom_call", output_to_operand_aliasing={{1}: (8, {})} | custom-call | bytes 20000000 | tf_op jit(solution)/shard_map/cond/branch_1_fun/pallas_call | solution.py:437
  138.4 4.7 %collective-permute-start.44 = (bf16[576,640]{1,0:T(8,128)(2,1)S(1)}, bf16[576,640]{1,0:T(8,128)(2,1)}, u32[]{:S(2)}, u32[]{:S(2)}) collective-permute-start(bf16[576,640]{1,0:T(8,128)(2,1)S(1)} %get-tuple-element.205), channel_id=1, source_target_pairs={{0,2},{1,3},{2,4},{3,5},{4,6},{5,7},{8,10},{9,11},{10,12},{11,13},... | collective-permute-start | bytes 2211848 | tf_op jit(solution)/shard_map/cond/branch_1_fun/ppermute | solution.py:483
  147.3 5.1 %collective-permute-start.42 = (bf16[576,640]{1,0:T(8,128)(2,1)S(1)}, bf16[576,640]{1,0:T(8,128)(2,1)S(1)}, u32[]{:S(2)}, u32[]{:S(2)}) collective-permute-start(bf16[576,640]{1,0:T(8,128)(2,1)S(1)} %get-tuple-element.203), channel_id=1, source_target_pairs={{0,2},{1,3},{2,4},{3,5},{4,6},{5,7},{8,10},{9,11},{10,12},{11,13},... | collective-permute-start | bytes 2211848 | tf_op jit(solution)/shard_map/cond/branch_1_fun/ppermute | solution.py:483
  152.4 6.6 %collective-permute-done.44.refs_1_ = bf16[576,640]{1,0:T(8,128)(2,1)} collective-permute-done((bf16[576,640]{1,0:T(8,128)(2,1)S(1)}, bf16[576,640]{1,0:T(8,128)(2,1)}, u32[]{:S(2)}, u32[]{:S(2)}) %collective-permute-start.44) | collective-permute-done | bytes 737312 | tf_op jit(solution)/shard_map/cond/branch_1_fun/ppermute | solution.py:483
  160.3 6.1 %branch_1_fun.25 = (f32[32,128,128]{2,1,0:T(8,128)S(1)}, bf16[21248,640]{1,0:T(8,128)(2,1)}) custom-call(s32[81]{0:T(128)S(1)} %get-tuple-element.160.loc_ref, s32[81]{0:T(128)S(1)} %get-tuple-element.161.when_ref, s32[81]{0:T(128)S(1)} %get-tuple-element.162.count_ref, s32[81]{0:T(128)S(1)} %get-tuple-element.163.target_ref, ...), custom_call_target="tpu_custom_call", output_to_operand_aliasing={{1}: (9, {})} | custom-call | bytes 20000000 | tf_op jit(solution)/shard_map/cond/branch_1_fun/pallas_call | solution.py:437
  167.0 4.1 %branch_1_fun.26 = (bf16[21248,640]{1,0:T(8,128)(2,1)}, bf16[576,640]{1,0:T(8,128)(2,1)}, bf16[576,640]{1,0:T(8,128)(2,1)}) custom-call(s32[2,5,3]{2,1,0:T(8,128)S(1)} %copy.219.runs_ref, bf16[10368,640]{1,0:T(8,128)(2,1)} %get-tuple-element.178.stream_ref, bf16[21248,640]{1,0:T(8,128)(2,1)} %get-tuple-element.208.refs_0_, ...), custom_call_target="tpu_custom_call", output_to_operand_aliasing={{0}: (2, {})} | custom-call | bytes 8847360 | tf_op jit(solution)/shard_map/cond/branch_1_fun/pallas_call | solution.py:494
  171.2 8.2 %collective-permute-start.50 = (bf16[576,640]{1,0:T(8,128)(2,1)}, bf16[576,640]{1,0:T(8,128)(2,1)}, u32[]{:S(2)}, u32[]{:S(2)}) collective-permute-start(bf16[576,640]{1,0:T(8,128)(2,1)} %get-tuple-element.220), channel_id=1, source_target_pairs={{0,2},{1,3},{2,4},{3,5},{4,6},{5,7},{8,10},{9,11},{10,12},{11,13},... | collective-permute-start | bytes 2211848 | tf_op jit(solution)/shard_map/cond/branch_1_fun/ppermute | solution.py:483
  186.3 4.6 %collective-permute-start.54 = (bf16[576,640]{1,0:T(8,128)(2,1)S(1)}, bf16[576,640]{1,0:T(8,128)(2,1)S(1)}, u32[]{:S(2)}, u32[]{:S(2)}) collective-permute-start(bf16[576,640]{1,0:T(8,128)(2,1)S(1)} %get-tuple-element.227), channel_id=1, source_target_pairs={{0,2},{1,3},{2,4},{3,5},{4,6},{5,7},{8,10},{9,11},{10,12},{11,13},... | collective-permute-start | bytes 2211848 | tf_op jit(solution)/shard_map/cond/branch_1_fun/ppermute | solution.py:483
  190.9 4.7 %collective-permute-done.50.refs_1_ = bf16[576,640]{1,0:T(8,128)(2,1)} collective-permute-done((bf16[576,640]{1,0:T(8,128)(2,1)}, bf16[576,640]{1,0:T(8,128)(2,1)}, u32[]{:S(2)}, u32[]{:S(2)}) %collective-permute-start.50) | collective-permute-done | bytes 737312 | tf_op jit(solution)/shard_map/cond/branch_1_fun/ppermute | solution.py:483
  196.9 9.0 %branch_1_fun.28 = (f32[32,128,128]{2,1,0:T(8,128)S(1)}, bf16[21248,640]{1,0:T(8,128)(2,1)}) custom-call(s32[81]{0:T(128)S(1)} %get-tuple-element.160.loc_ref, s32[81]{0:T(128)S(1)} %get-tuple-element.161.when_ref, s32[81]{0:T(128)S(1)} %get-tuple-element.162.count_ref, s32[81]{0:T(128)S(1)} %get-tuple-element.163.target_ref, ...), custom_call_target="tpu_custom_call", output_to_operand_aliasing={{1}: (9, {})} | custom-call | bytes 20000000 | tf_op jit(solution)/shard_map/cond/branch_1_fun/pallas_call | solution.py:437
  220.7 4.4 %branch_1_fun.33 = f32[32,128,128]{2,1,0:T(8,128)} custom-call(s32[81]{0:T(128)S(1)} %get-tuple-element.160.loc_ref, s32[81]{0:T(128)S(1)} %get-tuple-element.161.when_ref, s32[81]{0:T(128)S(1)} %get-tuple-element.162.count_ref, s32[81]{0:T(128)S(1)} %get-tuple-element.163.target_ref, f32[81]{0:T(128)S(1)} %get-tuple-element.164.coef_ref, ...), custom_call_target="tpu_custom_call" | custom-call | bytes 20000000 | tf_op jit(solution)/shard_map/cond/branch_1_fun/pallas_call | solution.py:437
  (240 shorter events, 74.2 us)
Async XLA Ops:
  43.1 35.9 %collective-permute-start.28 = (bf16[1152,640]{1,0:T(8,128)(2,1)}, bf16[1152,640]{1,0:T(8,128)(2,1)S(1)}, u32[]{:S(2)}, u32[]{:S(2)}) collective-permute-start(bf16[1152,640]{1,0:T(8,128)(2,1)} %get-tuple-element.171), channel_id=1, source_target_pairs={{0,2},{1,3},{2,4},{3,5},{4,6},{5,7},{8,10},{9,11},{10,12},{11,13},... | collective-permute-start | bytes 4423688 | tf_op jit(solution)/shard_map/cond/branch_1_fun/ppermute | solution.py:483
  46.7 36.4 %collective-permute-start.29 = (bf16[1152,640]{1,0:T(8,128)(2,1)}, bf16[1152,640]{1,0:T(8,128)(2,1)S(1)}, u32[]{:S(2)}, u32[]{:S(2)}) collective-permute-start(bf16[1152,640]{1,0:T(8,128)(2,1)} %get-tuple-element.172), channel_id=1, source_target_pairs={{2,0},{3,1},{4,2},{5,3},{6,4},{7,5},{10,8},{11,9},{12,10},{13,11},... | collective-permute-start | bytes 4423688 | tf_op jit(solution)/shard_map/cond/branch_1_fun/ppermute | solution.py:483
  60.7 120.9 %all-to-all-start.1 = ((bf16[4,1024,640]{2,1,0:T(8,128)(2,1)}), bf16[4,1024,640]{2,1,0:T(8,128)(2,1)}, u32[]{:S(2)}, u32[]{:S(2)}) async-start(bf16[4,1024,640]{2,1,0:T(8,128)(2,1)} %bitcast.296), calls=%async_computation.1 | async-start | bytes 10485760 | tf_op jit(solution)/shard_map/cond/branch_1_fun/all_to_all | solution.py:580
  83.1 28.2 %collective-permute-start.32 = (bf16[1152,640]{1,0:T(8,128)(2,1)S(1)}, bf16[1152,640]{1,0:T(8,128)(2,1)S(1)}, u32[]{:S(2)}, u32[]{:S(2)}) collective-permute-start(bf16[1152,640]{1,0:T(8,128)(2,1)S(1)} %collective-permute-done.28.refs_0_), channel_id=1, source_target_pairs={{0,1},{1,0},{2,3},{3,2},{4,5},{5,4},{6,7},{7,6},{8,9},{9,8},{10,11... | collective-permute-start | bytes 4423688 | tf_op jit(solution)/shard_map/cond/branch_1_fun/ppermute | solution.py:488
  83.1 28.7 %collective-permute-start.33 = (bf16[1152,640]{1,0:T(8,128)(2,1)S(1)}, bf16[1152,640]{1,0:T(8,128)(2,1)S(1)}, u32[]{:S(2)}, u32[]{:S(2)}) collective-permute-start(bf16[1152,640]{1,0:T(8,128)(2,1)S(1)} %collective-permute-done.29.refs_1_), channel_id=1, source_target_pairs={{0,1},{1,0},{2,3},{3,2},{4,5},{5,4},{6,7},{7,6},{8,9},{9,8},{10,11... | collective-permute-start | bytes 4423688 | tf_op jit(solution)/shard_map/cond/branch_1_fun/ppermute | solution.py:488
  86.6 21.4 %collective-permute-start.30 = (bf16[576,640]{1,0:T(8,128)(2,1)S(1)}, bf16[576,640]{1,0:T(8,128)(2,1)S(1)}, u32[]{:S(2)}, u32[]{:S(2)}) collective-permute-start(bf16[576,640]{1,0:T(8,128)(2,1)S(1)} %get-tuple-element.181), channel_id=1, source_target_pairs={{0,2},{1,3},{2,4},{3,5},{4,6},{5,7},{8,10},{9,11},{10,12},{11,13},... | collective-permute-start | bytes 2211848 | tf_op jit(solution)/shard_map/cond/branch_1_fun/ppermute | solution.py:483
  92.5 31.3 %collective-permute-start.36 = (bf16[576,640]{1,0:T(8,128)(2,1)S(1)}, bf16[576,640]{1,0:T(8,128)(2,1)S(1)}, u32[]{:S(2)}, u32[]{:S(2)}) collective-permute-start(bf16[576,640]{1,0:T(8,128)(2,1)S(1)} %get-tuple-element.191), channel_id=1, source_target_pairs={{0,2},{1,3},{2,4},{3,5},{4,6},{5,7},{8,10},{9,11},{10,12},{11,13},... | collective-permute-start | bytes 2211848 | tf_op jit(solution)/shard_map/cond/branch_1_fun/ppermute | solution.py:483
  108.0 27.5 %collective-permute-start.37 = (bf16[576,640]{1,0:T(8,128)(2,1)S(1)}, bf16[576,640]{1,0:T(8,128)(2,1)S(1)}, u32[]{:S(2)}, u32[]{:S(2)}) collective-permute-start(bf16[576,640]{1,0:T(8,128)(2,1)S(1)} %get-tuple-element.192), channel_id=1, source_target_pairs={{2,0},{3,1},{4,2},{5,3},{6,4},{7,5},{10,8},{11,9},{12,10},{13,11},... | collective-permute-start | bytes 2211848 | tf_op jit(solution)/shard_map/cond/branch_1_fun/ppermute | solution.py:483
  111.2 24.3 %collective-permute-start.38 = (bf16[576,640]{1,0:T(8,128)(2,1)S(1)}, bf16[576,640]{1,0:T(8,128)(2,1)S(1)}, u32[]{:S(2)}, u32[]{:S(2)}) collective-permute-start(bf16[576,640]{1,0:T(8,128)(2,1)S(1)} %collective-permute-done.30.refs_1_), channel_id=1, source_target_pairs={{0,1},{1,0},{2,3},{3,2},{4,5},{5,4},{6,7},{7,6},{8,9},{9,8},{10,11... | collective-permute-start | bytes 2211848 | tf_op jit(solution)/shard_map/cond/branch_1_fun/ppermute | solution.py:488
  111.3 24.8 %collective-permute-start.39 = (bf16[576,640]{1,0:T(8,128)(2,1)S(1)}, bf16[576,640]{1,0:T(8,128)(2,1)S(1)}, u32[]{:S(2)}, u32[]{:S(2)}) collective-permute-start(bf16[576,640]{1,0:T(8,128)(2,1)S(1)} %collective-permute-done.31.refs_2_), channel_id=1, source_target_pairs={{0,1},{1,0},{2,3},{3,2},{4,5},{5,4},{6,7},{7,6},{8,9},{9,8},{10,11... | collective-permute-start | bytes 2211848 | tf_op jit(solution)/shard_map/cond/branch_1_fun/ppermute | solution.py:488
  114.6 28.4 %collective-permute-start.34 = (bf16[576,640]{1,0:T(8,128)(2,1)S(1)}, bf16[576,640]{1,0:T(8,128)(2,1)S(1)}, u32[]{:S(2)}, u32[]{:S(2)}) collective-permute-start(bf16[576,640]{1,0:T(8,128)(2,1)S(1)} %get-tuple-element.189), channel_id=1, source_target_pairs={{0,2},{1,3},{2,4},{3,5},{4,6},{5,7},{8,10},{9,11},{10,12},{11,13},... | collective-permute-start | bytes 2211848 | tf_op jit(solution)/shard_map/cond/branch_1_fun/ppermute | solution.py:483
  123.8 20.6 %collective-permute-start.35 = (bf16[576,640]{1,0:T(8,128)(2,1)S(1)}, bf16[576,640]{1,0:T(8,128)(2,1)S(1)}, u32[]{:S(2)}, u32[]{:S(2)}) collective-permute-start(bf16[576,640]{1,0:T(8,128)(2,1)S(1)} %get-tuple-element.190), channel_id=1, source_target_pairs={{2,0},{3,1},{4,2},{5,3},{6,4},{7,5},{10,8},{11,9},{12,10},{13,11},... | collective-permute-start | bytes 2211848 | tf_op jit(solution)/shard_map/cond/branch_1_fun/ppermute | solution.py:483
  138.4 20.7 %collective-permute-start.44 = (bf16[576,640]{1,0:T(8,128)(2,1)S(1)}, bf16[576,640]{1,0:T(8,128)(2,1)}, u32[]{:S(2)}, u32[]{:S(2)}) collective-permute-start(bf16[576,640]{1,0:T(8,128)(2,1)S(1)} %get-tuple-element.205), channel_id=1, source_target_pairs={{0,2},{1,3},{2,4},{3,5},{4,6},{5,7},{8,10},{9,11},{10,12},{11,13},... | collective-permute-start | bytes 2211848 | tf_op jit(solution)/shard_map/cond/branch_1_fun/ppermute | solution.py:483
  143.1 23.4 %collective-permute-start.45 = (bf16[576,640]{1,0:T(8,128)(2,1)S(1)}, bf16[576,640]{1,0:T(8,128)(2,1)}, u32[]{:S(2)}, u32[]{:S(2)}) collective-permute-start(bf16[576,640]{1,0:T(8,128)(2,1)S(1)} %get-tuple-element.206), channel_id=1, source_target_pairs={{2,0},{3,1},{4,2},{5,3},{6,4},{7,5},{10,8},{11,9},{12,10},{13,11},... | collective-permute-start | bytes 2211848 | tf_op jit(solution)/shard_map/cond/branch_1_fun/ppermute | solution.py:483
  144.4 22.1 %collective-permute-start.46 = (bf16[576,640]{1,0:T(8,128)(2,1)S(1)}, bf16[576,640]{1,0:T(8,128)(2,1)S(1)}, u32[]{:S(2)}, u32[]{:S(2)}) collective-permute-start(bf16[576,640]{1,0:T(8,128)(2,1)S(1)} %collective-permute-done.34.refs_1_), channel_id=1, source_target_pairs={{0,1},{1,0},{2,3},{3,2},{4,5},{5,4},{6,7},{7,6},{8,9},{9,8},{10,11... | collective-permute-start | bytes 2211848 | tf_op jit(solution)/shard_map/cond/branch_1_fun/ppermute | solution.py:488
  144.5 22.6 %collective-permute-start.47 = (bf16[576,640]{1,0:T(8,128)(2,1)S(1)}, bf16[576,640]{1,0:T(8,128)(2,1)S(1)}, u32[]{:S(2)}, u32[]{:S(2)}) collective-permute-start(bf16[576,640]{1,0:T(8,128)(2,1)S(1)} %collective-permute-done.35.refs_2_), channel_id=1, source_target_pairs={{0,1},{1,0},{2,3},{3,2},{4,5},{5,4},{6,7},{7,6},{8,9},{9,8},{10,11... | collective-permute-start | bytes 2211848 | tf_op jit(solution)/shard_map/cond/branch_1_fun/ppermute | solution.py:488
  147.3 32.1 %collective-permute-start.42 = (bf16[576,640]{1,0:T(8,128)(2,1)S(1)}, bf16[576,640]{1,0:T(8,128)(2,1)S(1)}, u32[]{:S(2)}, u32[]{:S(2)}) collective-permute-start(bf16[576,640]{1,0:T(8,128)(2,1)S(1)} %get-tuple-element.203), channel_id=1, source_target_pairs={{0,2},{1,3},{2,4},{3,5},{4,6},{5,7},{8,10},{9,11},{10,12},{11,13},... | collective-permute-start | bytes 2211848 | tf_op jit(solution)/shard_map/cond/branch_1_fun/ppermute | solution.py:483
  159.0 20.4 %collective-permute-start.43 = (bf16[576,640]{1,0:T(8,128)(2,1)S(1)}, bf16[576,640]{1,0:T(8,128)(2,1)S(1)}, u32[]{:S(2)}, u32[]{:S(2)}) collective-permute-start(bf16[576,640]{1,0:T(8,128)(2,1)S(1)} %get-tuple-element.204), channel_id=1, source_target_pairs={{2,0},{3,1},{4,2},{5,3},{6,4},{7,5},{10,8},{11,9},{12,10},{13,11},... | collective-permute-start | bytes 2211848 | tf_op jit(solution)/shard_map/cond/branch_1_fun/ppermute | solution.py:483
  171.2 24.5 %collective-permute-start.50 = (bf16[576,640]{1,0:T(8,128)(2,1)}, bf16[576,640]{1,0:T(8,128)(2,1)}, u32[]{:S(2)}, u32[]{:S(2)}) collective-permute-start(bf16[576,640]{1,0:T(8,128)(2,1)} %get-tuple-element.220), channel_id=1, source_target_pairs={{0,2},{1,3},{2,4},{3,5},{4,6},{5,7},{8,10},{9,11},{10,12},{11,13},... | collective-permute-start | bytes 2211848 | tf_op jit(solution)/shard_map/cond/branch_1_fun/ppermute | solution.py:483
  180.3 25.7 %collective-permute-start.51 = (bf16[576,640]{1,0:T(8,128)(2,1)}, bf16[576,640]{1,0:T(8,128)(2,1)}, u32[]{:S(2)}, u32[]{:S(2)}) collective-permute-start(bf16[576,640]{1,0:T(8,128)(2,1)} %get-tuple-element.221), channel_id=1, source_target_pairs={{2,0},{3,1},{4,2},{5,3},{6,4},{7,5},{10,8},{11,9},{12,10},{13,11},... | collective-permute-start | bytes 2211848 | tf_op jit(solution)/shard_map/cond/branch_1_fun/ppermute | solution.py:483
  181.5 24.5 %collective-permute-start.52 = (bf16[576,640]{1,0:T(8,128)(2,1)S(1)}, bf16[576,640]{1,0:T(8,128)(2,1)}, u32[]{:S(2)}, u32[]{:S(2)}) collective-permute-start(bf16[576,640]{1,0:T(8,128)(2,1)S(1)} %collective-permute-done.42.refs_1_), channel_id=1, source_target_pairs={{0,1},{1,0},{2,3},{3,2},{4,5},{5,4},{6,7},{7,6},{8,9},{9,8},{10,11... | collective-permute-start | bytes 2211848 | tf_op jit(solution)/shard_map/cond/branch_1_fun/ppermute | solution.py:488
  181.6 24.9 %collective-permute-start.53 = (bf16[576,640]{1,0:T(8,128)(2,1)}, bf16[576,640]{1,0:T(8,128)(2,1)S(1)}, u32[]{:S(2)}, u32[]{:S(2)}) collective-permute-start(bf16[576,640]{1,0:T(8,128)(2,1)} %copy-done.9), channel_id=1, source_target_pairs={{0,1},{1,0},{2,3},{3,2},{4,5},{5,4},{6,7},{7,6},{8,9},{9,8},{10,11... | collective-permute-start | bytes 2211848 | tf_op jit(solution)/shard_map/cond/branch_1_fun/ppermute | solution.py:488
  186.3 26.6 %collective-permute-start.54 = (bf16[576,640]{1,0:T(8,128)(2,1)S(1)}, bf16[576,640]{1,0:T(8,128)(2,1)S(1)}, u32[]{:S(2)}, u32[]{:S(2)}) collective-permute-start(bf16[576,640]{1,0:T(8,128)(2,1)S(1)} %get-tuple-element.227), channel_id=1, source_target_pairs={{0,2},{1,3},{2,4},{3,5},{4,6},{5,7},{8,10},{9,11},{10,12},{11,13},... | collective-permute-start | bytes 2211848 | tf_op jit(solution)/shard_map/cond/branch_1_fun/ppermute | solution.py:483
  195.6 20.7 %collective-permute-start.55 = (bf16[576,640]{1,0:T(8,128)(2,1)S(1)}, bf16[576,640]{1,0:T(8,128)(2,1)S(1)}, u32[]{:S(2)}, u32[]{:S(2)}) collective-permute-start(bf16[576,640]{1,0:T(8,128)(2,1)S(1)} %get-tuple-element.228), channel_id=1, source_target_pairs={{2,0},{3,1},{4,2},{5,3},{6,4},{7,5},{10,8},{11,9},{12,10},{13,11},... | collective-permute-start | bytes 2211848 | tf_op jit(solution)/shard_map/cond/branch_1_fun/ppermute | solution.py:483
  (28 other events, 276.7 us)
